TPU v7x, 32 devices: a whole 2x2x4 slice. The times are simulated.
32 devices in a mesh: seq: 8 (over z, y), mp: 4 (over x, core).
Axes of the slice: x: 2, y: 2, z: 4, core: 2. Of those that a mesh axis runs over, the one named last changes fastest.
Arguments:
- inputs: bfloat16 [4, 4, 2048], replicated, may hold values from -3 to 3
- w_qkv: bfloat16 [3, 2048, 2048], P(None, None, 'mp'), may hold values from -0.125 to 0.125
- w_out: bfloat16 [2048, 2048], P('mp'), may hold values from -0.125 to 0.125
- w_gate_up: bfloat16 [2, 2048, 4096], P(None, None, 'mp'), may hold values from -0.125 to 0.125
- w_down: bfloat16 [4096, 2048], P('mp'), may hold values from -0.09375 to 0.09375
- cache_keys: bfloat16 [4, 1024, 2048], P(None, 'seq', 'mp'), may hold values from -256 to 256
- cache_values: bfloat16 [4, 1024, 2048], P(None, 'seq', 'mp'), may hold values from -6 to 6
- lengths: int32 [4], replicated, may hold values from 1 to 1024, as said below
Outputs:
- hidden: bfloat16 [4, 4, 2048], P(None, None, 'mp')
- queries: bfloat16 [4, 4, 2048], P(None, None, 'mp')
- new_keys: bfloat16 [4, 4, 2048], P(None, None, 'mp')
- new_values: bfloat16 [4, 4, 2048], P(None, None, 'mp')
Inputs may be any that keep to these rules, and one draw needn't show every extreme that they name: `lengths`: half of the 4 requests hold 1 to 64 cached positions, the others 1024 - 1024 // 8 to 1024; one request holds exactly 1024.
All inputs are finite; a program needn't handle non-finite values.
Results may differ from a plain program's by a relative error of at most 0.015.
The roundings to bfloat16 on the way count: a program that leaves them out, or rounds other values in their place, can miss the bound.
Values may be sent and summed in bfloat16 or wider, within the bound.
A program may use at most 128 MiB of HBM per device.

v0:
```python
import functools
import math

import jax
import jax.numpy as jnp
from jax import lax
from jax.experimental import pallas as pl
from jax.experimental.pallas import tpu as pltpu
from jax.sharding import PartitionSpec as P

DH = 128
NEG = -1e30
EPS = 1e-05
BASE = 10000.0
MESH = pl.DeviceIdType.MESH
F32 = jnp.float32
BF16 = jnp.bfloat16
QKV_CUTS = 4
HALVES = 2


def each(count, body):
    if count <= 8:
        for i in range(count):
            body(i)
    else:
        lax.fori_loop(0, count, lambda i, c: (body(i), c)[1], 0)


def iota(shape, axis):
    return lax.broadcasted_iota(jnp.int32, shape, axis)


def layer_norm(values):
    average = jnp.mean(values, axis=-1, keepdims=True)
    centred = values - average
    variance = jnp.mean(centred * centred, axis=-1, keepdims=True)
    return centred * lax.rsqrt(variance + EPS)


def split3(value):
    high = value.astype(BF16).astype(F32)
    middle = (value - high).astype(BF16).astype(F32)
    return [high, middle, value - high - middle]


def dot(a, b):
    return jnp.dot(a, b, preferred_element_type=F32)


def kernel(
    S, M,
    len_hbm, x_hbm, wqkv_hbm, wout_hbm, wgu_hbm, wdown_hbm, ck_hbm, cv_hbm,
    q_out, k_out, v_out, h_out,
    len_ref, x_in, qf, kf, vf, hf, wides, wqkv, wout, wgu, wdown, ck, cv,
    xf, send1, recv1, send2, recv2, send3, recv3, mids,
    xsem, qsem, wsem, csem, s1, r1, s2, r2, s3, r3,
):
    batch, steps, width = x_in.shape
    rows = batch * steps
    block = ck.shape[1]
    cols = wqkv.shape[2]
    heads = cols // DH
    own = rows // S
    pack = own * heads
    me = lax.axis_index("seq")
    mp = lax.axis_index("mp")

    x_copy = pltpu.make_async_copy(x_hbm, x_in, xsem.at[0])
    len_copy = pltpu.make_async_copy(len_hbm, len_ref, xsem.at[1])
    x_copy.start()
    len_copy.start()
    cut = width // QKV_CUTS
    q_copies = [
        [
            pltpu.make_async_copy(
                wqkv_hbm.at[j, pl.ds(c * cut, cut)], wqkv.at[j, pl.ds(c * cut, cut)], qsem.at[j, c]
            )
            for c in range(QKV_CUTS)
        ]
        for j in range(3)
    ]
    for c in range(QKV_CUTS):
        q_copies[0][c].start()
    ck_copy = pltpu.make_async_copy(ck_hbm, ck, csem.at[0])
    cv_copy = pltpu.make_async_copy(cv_hbm, cv, csem.at[1])
    ck_copy.start()
    cv_copy.start()
    out_copy = pltpu.make_async_copy(wout_hbm, wout, wsem.at[0])
    gate_copy = pltpu.make_async_copy(wgu_hbm.at[0], wgu.at[0], wsem.at[1])
    up_copy = pltpu.make_async_copy(wgu_hbm.at[1], wgu.at[1], wsem.at[2])
    down_copy = pltpu.make_async_copy(wdown_hbm, wdown, wsem.at[3])

    barrier = pltpu.get_barrier_semaphore()

    def greet(o):
        at = lax.rem(me * M + mp + 1 + o, S * M)
        pl.semaphore_signal(
            barrier, inc=1, device_id={"seq": at // M, "mp": lax.rem(at, M)}, device_id_type=MESH
        )

    if S * M <= 32:
        for o in range(S * M - 1):
            greet(o)
    else:
        each(S * M - 1, greet)

    x_copy.wait()
    for r in range(batch):
        xf[r * steps : (r + 1) * steps, :] = x_in[r].astype(F32)
    x = xf[...]
    normed = layer_norm(x).astype(BF16)

    def project(j):
        total = None
        for c in range(QKV_CUTS):
            q_copies[j][c].wait()
            if j == 0:
                q_copies[1][c].start()
                q_copies[2][c].start()
            term = dot(normed[:, c * cut : (c + 1) * cut], wqkv[j, c * cut : (c + 1) * cut, :])
            total = term if total is None else total + term
        return total

    len_copy.wait()
    token = iota((rows, DH), 0)
    position = lax.rem(token, steps)
    for r in range(batch):
        position = position + jnp.where(token // steps == r, len_ref[r], 0)
    lane = iota((rows, DH), 1)
    fold = lax.rem(lane, DH // 2).astype(F32)
    angle = position.astype(F32) * jnp.exp(fold * (-2.0 * math.log(BASE) / DH))
    cos = jnp.cos(angle)
    sin = jnp.sin(angle)
    sin = jnp.where(lane < DH // 2, -sin, sin)

    def rope(values, ref):
        for h in range(heads):
            v = values[:, h * DH : (h + 1) * DH]
            turned = pltpu.roll(v, DH // 2, 1)
            ref[:, h * DH : (h + 1) * DH] = (v * cos + turned * sin).astype(BF16).astype(F32)

    def emit(ref, out):
        for r in range(batch):
            out[r] = ref[r * steps : (r + 1) * steps, :].astype(BF16)

    rope(project(0), qf)

    full = rows * heads
    spread = (iota((full, rows), 0) // heads == iota((full, rows), 1)).astype(F32).astype(BF16)
    wide = dot(spread, qf[...].astype(BF16))
    own_cols = iota((full, cols), 1) // DH == lax.rem(iota((full, cols), 0), heads)
    wide = jnp.where(own_cols, wide, 0.0)
    wides[...] = wide.reshape(S, pack, cols)
    wide = wide.astype(BF16)

    nt = (((1,), (1,)), ((), ()))
    scale = DH ** -0.5
    group = steps * heads
    ck_copy.wait()
    out_copy.start()
    parts = []
    for r in range(batch):
        raw = lax.dot_general(
            wide[r * group : (r + 1) * group], ck[r], nt, preferred_element_type=F32
        )
        place = iota((group, block), 1) + me * block
        parts.append(jnp.where(place < len_ref[r], raw * scale, NEG))
    scores = jnp.concatenate(parts, axis=0)
    top = jnp.max(scores, axis=1, keepdims=True)
    weights = jnp.where(scores > 0.5 * NEG, jnp.exp(scores - top), 0.0)
    total = jnp.sum(weights, axis=1, keepdims=True)
    cv_copy.wait()
    gate_copy.start()
    weights = weights.astype(BF16)
    summed = jnp.concatenate(
        [dot(weights[r * group : (r + 1) * group], cv[r]) for r in range(batch)], axis=0
    )

    def by_head(wide_rows):
        head_of = lax.rem(iota((wide_rows.shape[0], DH), 0), heads)
        out = jnp.zeros((wide_rows.shape[0], DH), F32)
        for h in range(heads):
            out = out + jnp.where(head_of == h, wide_rows[:, h * DH : (h + 1) * DH], 0.0)
        return out

    spot = iota((full, DH), 1)
    stats = jnp.zeros((full, DH), F32)
    for i, piece in enumerate(split3(top) + split3(total)):
        stats = jnp.where(spot == i, piece, stats)
    send1[:, :, :DH] = by_head(summed).reshape(S, pack, DH).astype(BF16)
    send1[:, :, DH:] = stats.reshape(S, pack, DH).astype(BF16)

    pl.semaphore_wait(barrier, S * M - 1)

    def copy1(peer):
        return pltpu.make_async_remote_copy(
            send1.at[peer], recv1.at[me], s1.at[peer], r1.at[me],
            device_id={"seq": peer}, device_id_type=MESH,
        )

    def came(buf, src, send_sem, recv_sem, slot, axis):
        return pltpu.make_async_remote_copy(
            src, buf.at[slot], send_sem, recv_sem.at[slot],
            device_id={axis: slot}, device_id_type=MESH,
        )

    each(S - 1, lambda o: copy1(lax.rem(me + 1 + o, S)).start())
    recv1[me] = send1[me]

    up_copy.start()
    keys = project(1)
    down_copy.start()
    rope(keys, kf)
    values = project(2)
    vf[...] = values.astype(BF16).astype(F32)
    fresh = (
        lax.dot_general(
            wides[me].astype(BF16), kf[...].astype(BF16), nt, preferred_element_type=F32
        )
        * scale
    )
    row = me * pack + iota((pack, rows), 0)
    col = iota((pack, rows), 1)
    live = (row // group == col // steps) & (lax.rem(col, steps) <= lax.rem(row // heads, steps))
    fresh = jnp.where(live, fresh, NEG)
    fresh_top = jnp.max(fresh, axis=1, keepdims=True)
    fresh_w = jnp.where(live, jnp.exp(fresh - fresh_top), 0.0)
    fresh_total = jnp.sum(fresh_w, axis=1, keepdims=True)
    fresh_sum = by_head(dot(fresh_w.astype(BF16), vf[...].astype(BF16)))
    emit(qf, q_out)
    emit(kf, k_out)
    emit(vf, v_out)

    def wait1(o):
        peer = lax.rem(me + 1 + o, S)
        came(recv1, send1.at[peer], s1.at[peer], r1, peer, "seq").wait_recv()

    each(S - 1, wait1)
    stats = recv1[:, :, DH:].astype(F32)
    tops = stats[:, :, 0:1] + stats[:, :, 1:2] + stats[:, :, 2:3]
    sums = stats[:, :, 3:4] + stats[:, :, 4:5] + stats[:, :, 5:6]
    high = jnp.maximum(jnp.max(tops, axis=0), fresh_top)
    shrink = jnp.exp(tops - high[None])
    fresh_shrink = jnp.exp(fresh_top - high)
    whole = jnp.sum(sums * shrink, axis=0) + fresh_total * fresh_shrink
    context = jnp.sum(recv1[:, :, :DH].astype(F32) * shrink, axis=0) + fresh_sum * fresh_shrink
    context = context / whole
    context = context.astype(BF16).astype(F32)
    own_cols = iota((pack, cols), 1) // DH == lax.rem(iota((pack, cols), 0), heads)
    tiled = jnp.where(own_cols, jnp.concatenate([context] * heads, axis=1), 0.0)

    def lift(pieces, columns):
        at = iota((8, columns), 0)
        out = jnp.zeros((8, columns), F32)
        for i, piece in enumerate(pieces):
            out = jnp.where(at == i, piece, out)
        return out

    tiled_row = iota((pack, cols), 0) // heads
    flat = lift(
        [
            jnp.sum(jnp.where(tiled_row == i, tiled, 0.0), axis=0, keepdims=True)
            for i in range(own)
        ],
        cols,
    ).astype(BF16)
    out_copy.wait()
    half = width // HALVES

    def copy2(p, peer):
        return pltpu.make_async_remote_copy(
            send2.at[p], recv2.at[p, mp], s2.at[p, peer], r2.at[p, mp],
            device_id={"mp": peer}, device_id_type=MESH,
        )

    others = sorted(range(1, M), key=lambda o: abs(o - M // 2))
    for p in range(HALVES):
        send2[p] = dot(flat, wout[:, p * half : (p + 1) * half])[:own].astype(BF16)
        for o in others:
            copy2(p, lax.rem(mp + o, M)).start()
        recv2[p, mp] = send2[p]
    pick = (
        (iota((8, rows), 1) == me * own + iota((8, rows), 0)) & (iota((8, rows), 0) < own)
    ).astype(F32).astype(BF16)
    mine_x = dot(pick, x.astype(BF16))

    def landed2(p, peer):
        return pltpu.make_async_remote_copy(
            send2.at[p], recv2.at[p, peer], s2.at[p, peer], r2.at[p, peer],
            device_id={"mp": peer}, device_id_type=MESH,
        )

    lifted = []
    for p in range(HALVES):
        for o in others:
            landed2(p, lax.rem(mp + o, M)).wait_recv()
        attn = recv2[p, 0].astype(F32)
        for j in range(1, M):
            attn = attn + recv2[p, j].astype(F32)
        lifted.append(lift([attn[i : i + 1] for i in range(own)], half))
    middle = mine_x + jnp.concatenate(lifted, axis=1)
    normed_mid = layer_norm(middle).astype(BF16)
    for j in range(M):
        mids[j] = middle[:own, j * cols : (j + 1) * cols]
    gate_copy.wait()
    gate = dot(normed_mid, wgu[0])
    up_copy.wait()
    up = dot(normed_mid, wgu[1])
    active = (gate / (1.0 + jnp.exp(-gate)) * up).astype(BF16)
    down_copy.wait()

    def copy3(seq, j):
        return pltpu.make_async_remote_copy(
            send3.at[j], recv3.at[me, mp], s3.at[seq, j], r3.at[me, mp],
            device_id={"seq": seq, "mp": j}, device_id_type=MESH,
        )

    def came3(seq, j):
        return pltpu.make_async_remote_copy(
            send3.at[j], recv3.at[seq, j], s3.at[seq, j], r3.at[seq, j],
            device_id={"seq": seq, "mp": j}, device_id_type=MESH,
        )

    def down_block(j):
        return dot(active, wdown[:, pl.ds(pl.multiple_of(j * cols, cols), cols)])[:own]

    def all_blocks(act):
        for o in others:
            j = lax.rem(mp + o, M)
            each(S, lambda i: act(lax.rem(me + S // 2 + i, S), j))
        each(S - 1, lambda i: act(lax.rem(me + 1 + i, S), mp))

    for o in others:
        j = lax.rem(mp + o, M)
        send3[j] = down_block(j).astype(BF16)
        each(S, lambda i: copy3(lax.rem(me + S // 2 + i, S), j).start())
    send3[mp] = (down_block(mp) + mids[mp]).astype(BF16)
    each(S - 1, lambda i: copy3(lax.rem(me + 1 + i, S), mp).start())
    recv3[me, mp] = send3[mp]
    all_blocks(lambda seq, j: came3(seq, j).wait_recv())
    for i in range(S):
        hidden = recv3[i, 0].astype(F32)
        for j in range(1, M):
            hidden = hidden + recv3[i, j].astype(F32)
        hf[i * own : (i + 1) * own, :] = hidden
    emit(hf, h_out)

    each(S - 1, lambda o: copy1(lax.rem(me + 1 + o, S)).wait_send())
    for p in range(HALVES):
        for o in others:
            copy2(p, lax.rem(mp + o, M)).wait_send()
    all_blocks(lambda seq, j: copy3(seq, j).wait_send())


def deliver(*refs):
    sems = refs[-1]
    count = len(refs) // 2
    copies = [
        pltpu.make_async_copy(refs[i], refs[count + i], sems.at[i]) for i in range(count)
    ]
    for copy in copies:
        copy.start()
    for copy in copies:
        copy.wait()


def per_device(S, M, inputs, w_qkv, w_out, w_gate_up, w_down, cache_keys, cache_values, lengths):
    batch, steps, width = inputs.shape
    rows = batch * steps
    cols = w_qkv.shape[2]
    heads = cols // DH
    own = rows // S
    pack = own * heads
    anywhere = pl.BlockSpec(memory_space=pl.ANY)
    vmem = pl.BlockSpec(memory_space=pltpu.VMEM)
    shape = (batch, steps, cols)
    small = pltpu.VMEM((rows, cols), F32)
    dma = pltpu.SemaphoreType.DMA
    results = pl.pallas_call(
        functools.partial(kernel, S, M),
        out_shape=[pltpu.VMEM(shape, BF16)] * 4,
        in_specs=[anywhere] * 8,
        out_specs=[vmem] * 4,
        scratch_shapes=[
            pltpu.SMEM(lengths.shape, jnp.int32),
            pltpu.VMEM(inputs.shape, BF16),
            small,
            small,
            small,
            small,
            pltpu.VMEM((S, pack, cols), F32),
            pltpu.VMEM(w_qkv.shape, BF16),
            pltpu.VMEM(w_out.shape, BF16),
            pltpu.VMEM(w_gate_up.shape, BF16),
            pltpu.VMEM(w_down.shape, BF16),
            pltpu.VMEM(cache_keys.shape, BF16),
            pltpu.VMEM(cache_values.shape, BF16),
            pltpu.VMEM((rows, width), F32),
            pltpu.VMEM((S, pack, 2 * DH), BF16),
            pltpu.VMEM((S, pack, 2 * DH), BF16),
            pltpu.VMEM((HALVES, own, width // HALVES), BF16),
            pltpu.VMEM((HALVES, M, own, width // HALVES), BF16),
            pltpu.VMEM((M, own, cols), BF16),
            pltpu.VMEM((S, M, own, cols), BF16),
            pltpu.VMEM((M, own, cols), F32),
            dma((2,)),
            dma((3, QKV_CUTS)),
            dma((4,)),
            dma((2,)),
            dma((S,)),
            dma((S,)),
            dma((HALVES, M)),
            dma((HALVES, M)),
            dma((S, M)),
            dma((S, M)),
        ],
        compiler_params=pltpu.CompilerParams(
            collective_id=0, has_side_effects=True, vmem_limit_bytes=60 * 1024 * 1024
        ),
        name="layer",
    )(lengths, inputs, w_qkv, w_out, w_gate_up, w_down, cache_keys, cache_values)
    queries, keys, values, hidden = (
        pltpu.with_memory_space_constraint(a, pltpu.VMEM) for a in results
    )
    return tuple(
        pl.pallas_call(
            deliver,
            out_shape=[jax.ShapeDtypeStruct(shape, BF16)] * 4,
            in_specs=[vmem] * 4,
            out_specs=[anywhere] * 4,
            scratch_shapes=[dma((4,))],
            name="deliver",
        )(hidden, queries, keys, values)
    )


def solution(mesh):
    cut = P(None, None, "mp")
    cache = P(None, "seq", "mp")
    return jax.shard_map(
        functools.partial(per_device, mesh.shape["seq"], mesh.shape["mp"]),
        mesh=mesh,
        in_specs=(P(), cut, P("mp", None), cut, P("mp", None), cache, cache, P()),
        out_specs=(cut,) * 4,
        check_vma=False,
    )
```

profile of v0, /device:TPU:0, one launch (start us, length us, event | category | flops | bytes accessed | tf_op | source)
XLA Modules:
  0.0 23.4 jit_solution(12381285412983957864)
XLA Ops:
  0.6 22.1 %layer.1 = (bf16[4,4,512]{2,1,0:T(4,128)(2,1)S(1)}, bf16[4,4,512]{2,1,0:T(4,128)(2,1)S(1)}, bf16[4,4,512]{2,1,0:T(4,128)(2,1)S(1)}, bf16[4,4,512]{2,1,0:T(4,128)(2,1)S(1)}) custom-call(s32[4]{0:T(128)} %len_hbm.1, bf16[4,4,2048]{2,1,0:T(4,128)(2,1)} %x_hbm.1, bf16[3,2048,512]{2,1,0:T(8,128)(2,1)} %wqkv_hbm.1, bf16[512,2048]{1,0:T(8,128)(2,1)} %wout_hbm.1, ...), custom_call_target="tpu_custom_call" | custom-call | tf_op jit(solution)/shard_map/layer/pallas_call | solution.py:380
  22.8 0.7 %deliver.1 = (bf16[4,4,512]{2,1,0:T(4,128)(2,1)}, bf16[4,4,512]{2,1,0:T(4,128)(2,1)}, bf16[4,4,512]{2,1,0:T(4,128)(2,1)}, bf16[4,4,512]{2,1,0:T(4,128)(2,1)}) custom-call(bf16[4,4,512]{2,1,0:T(4,128)(2,1)S(1)} %get-tuple-element.8.refs_0_, bf16[4,4,512]{2,1,0:T(4,128)(2,1)S(1)} %get-tuple-element.9.refs_1_, ...), custom_call_target="tpu_custom_call" | custom-call | tf_op jit(solution)/shard_map/deliver/pallas_call | solution.py:427
where the time goes:
time: 23.6 us; the launch traced here: 23.4 us
  Pallas kernels  22.8 us (97%)
  between operations  0.64 us (3%)
    pallas_call x1, Pallas kernels, per_device(): pl.pallas_call(functools.partial(kernel, S, M), out_shape=[pltpu.VMEM(sha...  22.1 us
    pallas_call x1, Pallas kernels, per_device(): pl.pallas_call(deliver, out_shape=[jax.ShapeDtypeStruct(shape, BF16)] * 4...  0.66 us

commit v1 on v0

--- a/solution.py
+++ b/solution.py
@@ -17,6 +17,7 @@
 BF16 = jnp.bfloat16
 QKV_CUTS = 4
 HALVES = 2
+PAIR = 2
 
 
 def each(count, body):
@@ -63,8 +64,13 @@
     heads = cols // DH
     own = rows // S
     pack = own * heads
+    team = own * PAIR
+    few = heads // PAIR
+    hidden_units = wdown.shape[0]
     me = lax.axis_index("seq")
     mp = lax.axis_index("mp")
+    unit = lax.rem(me, PAIR)
+    first = me - unit
 
     x_copy = pltpu.make_async_copy(x_hbm, x_in, xsem.at[0])
     len_copy = pltpu.make_async_copy(len_hbm, len_ref, xsem.at[1])
@@ -86,10 +92,15 @@
     cv_copy = pltpu.make_async_copy(cv_hbm, cv, csem.at[1])
     ck_copy.start()
     cv_copy.start()
-    out_copy = pltpu.make_async_copy(wout_hbm, wout, wsem.at[0])
-    gate_copy = pltpu.make_async_copy(wgu_hbm.at[0], wgu.at[0], wsem.at[1])
-    up_copy = pltpu.make_async_copy(wgu_hbm.at[1], wgu.at[1], wsem.at[2])
-    down_copy = pltpu.make_async_copy(wdown_hbm, wdown, wsem.at[3])
+    unit_cols = pl.ds(pl.multiple_of(unit * hidden_units, hidden_units), hidden_units)
+    out_copy = pltpu.make_async_copy(
+        wout_hbm.at[pl.ds(unit * few * DH, few * DH)], wout, wsem.at[0])
+    gate_copy = pltpu.make_async_copy(
+        wgu_hbm.at[0, :, unit_cols], wgu.at[0], wsem.at[1])
+    up_copy = pltpu.make_async_copy(
+        wgu_hbm.at[1, :, unit_cols], wgu.at[1], wsem.at[2])
+    down_copy = pltpu.make_async_copy(
+        wdown_hbm.at[pl.ds(unit * hidden_units, hidden_units)], wdown, wsem.at[3])
 
     barrier = pltpu.get_barrier_semaphore()
 
@@ -147,9 +158,16 @@
     rope(project(0), qf)
 
     full = rows * heads
-    spread = (iota((full, rows), 0) // heads == iota((full, rows), 1)).astype(F32).astype(BF16)
+
+    def token_of(row):
+        return row // (PAIR * pack) * team + lax.rem(row, pack) // few
+
+    def head_of(row):
+        return lax.rem(row // pack, PAIR) * few + lax.rem(row, few)
+
+    spread = (token_of(iota((full, rows), 0)) == iota((full, rows), 1)).astype(F32).astype(BF16)
     wide = dot(spread, qf[...].astype(BF16))
-    own_cols = iota((full, cols), 1) // DH == lax.rem(iota((full, cols), 0), heads)
+    own_cols = iota((full, cols), 1) // DH == head_of(iota((full, cols), 0))
     wide = jnp.where(own_cols, wide, 0.0)
     wides[...] = wide.reshape(S, pack, cols)
     wide = wide.astype(BF16)
@@ -177,18 +195,18 @@
         [dot(weights[r * group : (r + 1) * group], cv[r]) for r in range(batch)], axis=0
     )
 
-    def by_head(wide_rows):
-        head_of = lax.rem(iota((wide_rows.shape[0], DH), 0), heads)
+    def by_head(wide_rows, start):
+        head = head_of(start + iota((wide_rows.shape[0], DH), 0))
         out = jnp.zeros((wide_rows.shape[0], DH), F32)
         for h in range(heads):
-            out = out + jnp.where(head_of == h, wide_rows[:, h * DH : (h + 1) * DH], 0.0)
+            out = out + jnp.where(head == h, wide_rows[:, h * DH : (h + 1) * DH], 0.0)
         return out
 
     spot = iota((full, DH), 1)
     stats = jnp.zeros((full, DH), F32)
     for i, piece in enumerate(split3(top) + split3(total)):
         stats = jnp.where(spot == i, piece, stats)
-    send1[:, :, :DH] = by_head(summed).reshape(S, pack, DH).astype(BF16)
+    send1[:, :, :DH] = by_head(summed, 0).reshape(S, pack, DH).astype(BF16)
     send1[:, :, DH:] = stats.reshape(S, pack, DH).astype(BF16)
 
     pl.semaphore_wait(barrier, S * M - 1)
@@ -220,14 +238,14 @@
         )
         * scale
     )
-    row = me * pack + iota((pack, rows), 0)
+    row = token_of(me * pack + iota((pack, rows), 0))
     col = iota((pack, rows), 1)
-    live = (row // group == col // steps) & (lax.rem(col, steps) <= lax.rem(row // heads, steps))
+    live = (row // steps == col // steps) & (col <= row)
     fresh = jnp.where(live, fresh, NEG)
     fresh_top = jnp.max(fresh, axis=1, keepdims=True)
     fresh_w = jnp.where(live, jnp.exp(fresh - fresh_top), 0.0)
     fresh_total = jnp.sum(fresh_w, axis=1, keepdims=True)
-    fresh_sum = by_head(dot(fresh_w.astype(BF16), vf[...].astype(BF16)))
+    fresh_sum = by_head(dot(fresh_w.astype(BF16), vf[...].astype(BF16)), me * pack)
     emit(qf, q_out)
     emit(kf, k_out)
     emit(vf, v_out)
@@ -247,8 +265,9 @@
     context = jnp.sum(recv1[:, :, :DH].astype(F32) * shrink, axis=0) + fresh_sum * fresh_shrink
     context = context / whole
     context = context.astype(BF16).astype(F32)
-    own_cols = iota((pack, cols), 1) // DH == lax.rem(iota((pack, cols), 0), heads)
-    tiled = jnp.where(own_cols, jnp.concatenate([context] * heads, axis=1), 0.0)
+    part_cols = few * DH
+    own_cols = iota((pack, part_cols), 1) // DH == lax.rem(iota((pack, part_cols), 0), few)
+    tiled = jnp.where(own_cols, jnp.concatenate([context] * few, axis=1), 0.0)
 
     def lift(pieces, columns):
         at = iota((8, columns), 0)
@@ -257,52 +276,56 @@
             out = jnp.where(at == i, piece, out)
         return out
 
-    tiled_row = iota((pack, cols), 0) // heads
+    tiled_row = iota((pack, part_cols), 0) // few
     flat = lift(
         [
             jnp.sum(jnp.where(tiled_row == i, tiled, 0.0), axis=0, keepdims=True)
-            for i in range(own)
+            for i in range(team)
         ],
-        cols,
+        part_cols,
     ).astype(BF16)
     out_copy.wait()
     half = width // HALVES
 
-    def copy2(p, peer):
-        return pltpu.make_async_remote_copy(
-            send2.at[p], recv2.at[p, mp], s2.at[p, peer], r2.at[p, mp],
-            device_id={"mp": peer}, device_id_type=MESH,
+    def copy2(p, u, j):
+        return pltpu.make_async_remote_copy(
+            send2.at[p], recv2.at[p, unit, mp], s2.at[p, u, j], r2.at[p, unit, mp],
+            device_id={"seq": first + u, "mp": j}, device_id_type=MESH,
         )
 
     others = sorted(range(1, M), key=lambda o: abs(o - M // 2))
+    near = [(v, o) for v in range(PAIR - 1, -1, -1) for o in others] + [(v, 0) for v in range(1, PAIR)]
+    near = [(lax.rem(unit + v, PAIR), lax.rem(mp + o, M)) for v, o in near]
     for p in range(HALVES):
-        send2[p] = dot(flat, wout[:, p * half : (p + 1) * half])[:own].astype(BF16)
-        for o in others:
-            copy2(p, lax.rem(mp + o, M)).start()
-        recv2[p, mp] = send2[p]
+        send2[p] = dot(flat, wout[:, p * half : (p + 1) * half])[:team].astype(BF16)
+        for u, j in near:
+            copy2(p, u, j).start()
+        recv2[p, unit, mp] = send2[p]
     pick = (
-        (iota((8, rows), 1) == me * own + iota((8, rows), 0)) & (iota((8, rows), 0) < own)
+        (iota((8, rows), 1) == first * own + iota((8, rows), 0))
+        & (iota((8, rows), 0) < team)
     ).astype(F32).astype(BF16)
     mine_x = dot(pick, x.astype(BF16))
 
-    def landed2(p, peer):
-        return pltpu.make_async_remote_copy(
-            send2.at[p], recv2.at[p, peer], s2.at[p, peer], r2.at[p, peer],
-            device_id={"mp": peer}, device_id_type=MESH,
+    def landed2(p, u, j):
+        return pltpu.make_async_remote_copy(
+            send2.at[p], recv2.at[p, u, j], s2.at[p, u, j], r2.at[p, u, j],
+            device_id={"seq": first + u, "mp": j}, device_id_type=MESH,
         )
 
     lifted = []
     for p in range(HALVES):
-        for o in others:
-            landed2(p, lax.rem(mp + o, M)).wait_recv()
-        attn = recv2[p, 0].astype(F32)
-        for j in range(1, M):
-            attn = attn + recv2[p, j].astype(F32)
-        lifted.append(lift([attn[i : i + 1] for i in range(own)], half))
+        for u, j in near:
+            landed2(p, u, j).wait_recv()
+        attn = jnp.zeros((team, half), F32)
+        for u in range(PAIR):
+            for j in range(M):
+                attn = attn + recv2[p, u, j].astype(F32)
+        lifted.append(lift([attn[i : i + 1] for i in range(team)], half))
     middle = mine_x + jnp.concatenate(lifted, axis=1)
     normed_mid = layer_norm(middle).astype(BF16)
     for j in range(M):
-        mids[j] = middle[:own, j * cols : (j + 1) * cols]
+        mids[j] = jnp.where(unit == 0, middle[:team, j * cols : (j + 1) * cols], 0.0)
     gate_copy.wait()
     gate = dot(normed_mid, wgu[0])
     up_copy.wait()
@@ -323,7 +346,7 @@
         )
 
     def down_block(j):
-        return dot(active, wdown[:, pl.ds(pl.multiple_of(j * cols, cols), cols)])[:own]
+        return dot(active, wdown[:, pl.ds(pl.multiple_of(j * cols, cols), cols)])[:team]
 
     def all_blocks(act):
         for o in others:
@@ -339,17 +362,18 @@
     each(S - 1, lambda i: copy3(lax.rem(me + 1 + i, S), mp).start())
     recv3[me, mp] = send3[mp]
     all_blocks(lambda seq, j: came3(seq, j).wait_recv())
-    for i in range(S):
-        hidden = recv3[i, 0].astype(F32)
-        for j in range(1, M):
-            hidden = hidden + recv3[i, j].astype(F32)
-        hf[i * own : (i + 1) * own, :] = hidden
+    for i in range(S // PAIR):
+        hidden = jnp.zeros((team, cols), F32)
+        for u in range(PAIR):
+            for j in range(M):
+                hidden = hidden + recv3[i * PAIR + u, j].astype(F32)
+        hf[i * team : (i + 1) * team, :] = hidden
     emit(hf, h_out)
 
     each(S - 1, lambda o: copy1(lax.rem(me + 1 + o, S)).wait_send())
     for p in range(HALVES):
-        for o in others:
-            copy2(p, lax.rem(mp + o, M)).wait_send()
+        for u, j in near:
+            copy2(p, u, j).wait_send()
     all_blocks(lambda seq, j: copy3(seq, j).wait_send())
 
 
@@ -372,6 +396,8 @@
     heads = cols // DH
     own = rows // S
     pack = own * heads
+    team = own * PAIR
+    units = w_down.shape[0] // PAIR
     anywhere = pl.BlockSpec(memory_space=pl.ANY)
     vmem = pl.BlockSpec(memory_space=pltpu.VMEM)
     shape = (batch, steps, cols)
@@ -391,27 +417,27 @@
             small,
             pltpu.VMEM((S, pack, cols), F32),
             pltpu.VMEM(w_qkv.shape, BF16),
-            pltpu.VMEM(w_out.shape, BF16),
-            pltpu.VMEM(w_gate_up.shape, BF16),
-            pltpu.VMEM(w_down.shape, BF16),
+            pltpu.VMEM((cols // PAIR, width), BF16),
+            pltpu.VMEM((2, width, units), BF16),
+            pltpu.VMEM((units, width), BF16),
             pltpu.VMEM(cache_keys.shape, BF16),
             pltpu.VMEM(cache_values.shape, BF16),
             pltpu.VMEM((rows, width), F32),
             pltpu.VMEM((S, pack, 2 * DH), BF16),
             pltpu.VMEM((S, pack, 2 * DH), BF16),
-            pltpu.VMEM((HALVES, own, width // HALVES), BF16),
-            pltpu.VMEM((HALVES, M, own, width // HALVES), BF16),
-            pltpu.VMEM((M, own, cols), BF16),
-            pltpu.VMEM((S, M, own, cols), BF16),
-            pltpu.VMEM((M, own, cols), F32),
+            pltpu.VMEM((HALVES, team, width // HALVES), BF16),
+            pltpu.VMEM((HALVES, PAIR, M, team, width // HALVES), BF16),
+            pltpu.VMEM((M, team, cols), BF16),
+            pltpu.VMEM((S, M, team, cols), BF16),
+            pltpu.VMEM((M, team, cols), F32),
             dma((2,)),
             dma((3, QKV_CUTS)),
             dma((4,)),
             dma((2,)),
             dma((S,)),
             dma((S,)),
-            dma((HALVES, M)),
-            dma((HALVES, M)),
+            dma((HALVES, PAIR, M)),
+            dma((HALVES, PAIR, M)),
             dma((S, M)),
             dma((S, M)),
         ],

time: 23.6 us -> 23.7 us (level)
  no operation moved by 1% of the time
where the time goes in v1:
time: 23.7 us; the launch traced here: 23.5 us
  Pallas kernels  22.9 us (97%)
  between operations  0.64 us (3%)
    pallas_call x1, Pallas kernels, per_device(): pl.pallas_call(functools.partial(kernel, S, M), out_shape=[pltpu.VMEM(sha...  22.2 us
    pallas_call x1, Pallas kernels, per_device(): pl.pallas_call(deliver, out_shape=[jax.ShapeDtypeStruct(shape, BF16)] * 4...  0.66 us

profile of v1, /device:TPU:0, one launch (start us, length us, event | category | flops | bytes accessed | tf_op | source)
XLA Modules:
  0.0 23.5 jit_solution(2566211779099993872)
XLA Ops:
  0.6 22.2 %layer.1 = (bf16[4,4,512]{2,1,0:T(4,128)(2,1)S(1)}, bf16[4,4,512]{2,1,0:T(4,128)(2,1)S(1)}, bf16[4,4,512]{2,1,0:T(4,128)(2,1)S(1)}, bf16[4,4,512]{2,1,0:T(4,128)(2,1)S(1)}) custom-call(s32[4]{0:T(128)} %len_hbm.1, bf16[4,4,2048]{2,1,0:T(4,128)(2,1)} %x_hbm.1, bf16[3,2048,512]{2,1,0:T(8,128)(2,1)} %wqkv_hbm.1, bf16[512,2048]{1,0:T(8,128)(2,1)} %wout_hbm.1, ...), custom_call_target="tpu_custom_call" | custom-call | tf_op jit(solution)/shard_map/layer/pallas_call | solution.py:406
  22.8 0.7 %deliver.1 = (bf16[4,4,512]{2,1,0:T(4,128)(2,1)}, bf16[4,4,512]{2,1,0:T(4,128)(2,1)}, bf16[4,4,512]{2,1,0:T(4,128)(2,1)}, bf16[4,4,512]{2,1,0:T(4,128)(2,1)}) custom-call(bf16[4,4,512]{2,1,0:T(4,128)(2,1)S(1)} %get-tuple-element.8.refs_0_, bf16[4,4,512]{2,1,0:T(4,128)(2,1)S(1)} %get-tuple-element.9.refs_1_, ...), custom_call_target="tpu_custom_call" | custom-call | tf_op jit(solution)/shard_map/deliver/pallas_call | solution.py:453

commit v2 on v1

--- a/solution.py
+++ b/solution.py
@@ -30,6 +30,14 @@
 
 def iota(shape, axis):
     return lax.broadcasted_iota(jnp.int32, shape, axis)
+
+
+def over(value, by):
+    return value >> (by.bit_length() - 1) if by & (by - 1) == 0 else lax.div(value, by)
+
+
+def mod(value, by):
+    return value & (by - 1) if by & (by - 1) == 0 else lax.rem(value, by)
 
 
 def layer_norm(values):
@@ -74,8 +82,8 @@
 
     x_copy = pltpu.make_async_copy(x_hbm, x_in, xsem.at[0])
     len_copy = pltpu.make_async_copy(len_hbm, len_ref, xsem.at[1])
+    len_copy.start()
     x_copy.start()
-    len_copy.start()
     cut = width // QKV_CUTS
     q_copies = [
         [
@@ -116,6 +124,18 @@
     else:
         each(S * M - 1, greet)
 
+    len_copy.wait()
+    token = iota((rows, DH), 0)
+    position = mod(token, steps)
+    for r in range(batch):
+        position = position + jnp.where(over(token, steps) == r, len_ref[r], 0)
+    lane = iota((rows, DH), 1)
+    fold = mod(lane, DH // 2).astype(F32)
+    angle = position.astype(F32) * jnp.exp(fold * (-2.0 * math.log(BASE) / DH))
+    cos = jnp.cos(angle)
+    sin = jnp.sin(angle)
+    sin = jnp.where(lane < DH // 2, -sin, sin)
+
     x_copy.wait()
     for r in range(batch):
         xf[r * steps : (r + 1) * steps, :] = x_in[r].astype(F32)
@@ -133,18 +153,6 @@
             total = term if total is None else total + term
         return total
 
-    len_copy.wait()
-    token = iota((rows, DH), 0)
-    position = lax.rem(token, steps)
-    for r in range(batch):
-        position = position + jnp.where(token // steps == r, len_ref[r], 0)
-    lane = iota((rows, DH), 1)
-    fold = lax.rem(lane, DH // 2).astype(F32)
-    angle = position.astype(F32) * jnp.exp(fold * (-2.0 * math.log(BASE) / DH))
-    cos = jnp.cos(angle)
-    sin = jnp.sin(angle)
-    sin = jnp.where(lane < DH // 2, -sin, sin)
-
     def rope(values, ref):
         for h in range(heads):
             v = values[:, h * DH : (h + 1) * DH]
@@ -160,14 +168,14 @@
     full = rows * heads
 
     def token_of(row):
-        return row // (PAIR * pack) * team + lax.rem(row, pack) // few
+        return over(row, PAIR * pack) * team + over(mod(row, pack), few)
 
     def head_of(row):
-        return lax.rem(row // pack, PAIR) * few + lax.rem(row, few)
-
-    spread = (token_of(iota((full, rows), 0)) == iota((full, rows), 1)).astype(F32).astype(BF16)
+        return mod(over(row, pack), PAIR) * few + mod(row, few)
+
+    spread = (token_of(iota((full, 1), 0)) == iota((full, rows), 1)).astype(F32).astype(BF16)
     wide = dot(spread, qf[...].astype(BF16))
-    own_cols = iota((full, cols), 1) // DH == head_of(iota((full, cols), 0))
+    own_cols = over(iota((full, cols), 1), DH) == head_of(iota((full, 1), 0))
     wide = jnp.where(own_cols, wide, 0.0)
     wides[...] = wide.reshape(S, pack, cols)
     wide = wide.astype(BF16)
@@ -196,7 +204,7 @@
     )
 
     def by_head(wide_rows, start):
-        head = head_of(start + iota((wide_rows.shape[0], DH), 0))
+        head = head_of(start + iota((wide_rows.shape[0], 1), 0))
         out = jnp.zeros((wide_rows.shape[0], DH), F32)
         for h in range(heads):
             out = out + jnp.where(head == h, wide_rows[:, h * DH : (h + 1) * DH], 0.0)
@@ -238,17 +246,14 @@
         )
         * scale
     )
-    row = token_of(me * pack + iota((pack, rows), 0))
+    row = token_of(me * pack + iota((pack, 1), 0))
     col = iota((pack, rows), 1)
-    live = (row // steps == col // steps) & (col <= row)
+    live = (over(row, steps) == over(col, steps)) & (col <= row)
     fresh = jnp.where(live, fresh, NEG)
     fresh_top = jnp.max(fresh, axis=1, keepdims=True)
     fresh_w = jnp.where(live, jnp.exp(fresh - fresh_top), 0.0)
     fresh_total = jnp.sum(fresh_w, axis=1, keepdims=True)
     fresh_sum = by_head(dot(fresh_w.astype(BF16), vf[...].astype(BF16)), me * pack)
-    emit(qf, q_out)
-    emit(kf, k_out)
-    emit(vf, v_out)
 
     def wait1(o):
         peer = lax.rem(me + 1 + o, S)
@@ -266,7 +271,7 @@
     context = context / whole
     context = context.astype(BF16).astype(F32)
     part_cols = few * DH
-    own_cols = iota((pack, part_cols), 1) // DH == lax.rem(iota((pack, part_cols), 0), few)
+    own_cols = over(iota((pack, part_cols), 1), DH) == mod(iota((pack, 1), 0), few)
     tiled = jnp.where(own_cols, jnp.concatenate([context] * few, axis=1), 0.0)
 
     def lift(pieces, columns):
@@ -276,7 +281,7 @@
             out = jnp.where(at == i, piece, out)
         return out
 
-    tiled_row = iota((pack, part_cols), 0) // few
+    tiled_row = over(iota((pack, part_cols), 0), few)
     flat = lift(
         [
             jnp.sum(jnp.where(tiled_row == i, tiled, 0.0), axis=0, keepdims=True)
@@ -361,6 +366,9 @@
     send3[mp] = (down_block(mp) + mids[mp]).astype(BF16)
     each(S - 1, lambda i: copy3(lax.rem(me + 1 + i, S), mp).start())
     recv3[me, mp] = send3[mp]
+    emit(qf, q_out)
+    emit(kf, k_out)
+    emit(vf, v_out)
     all_blocks(lambda seq, j: came3(seq, j).wait_recv())
     for i in range(S // PAIR):
         hidden = jnp.zeros((team, cols), F32)

time: 23.7 us -> 23.8 us (level)
  no operation moved by 1% of the time
where the time goes in v2:
time: 23.8 us; the launch traced here: 23.7 us
  Pallas kernels  23 us (97%)
  between operations  0.64 us (3%)
    pallas_call x1, Pallas kernels, per_device(): pl.pallas_call(functools.partial(kernel, S, M), out_shape=[pltpu.VMEM(sha...  22.4 us
    pallas_call x1, Pallas kernels, per_device(): pl.pallas_call(deliver, out_shape=[jax.ShapeDtypeStruct(shape, BF16)] * 4...  0.66 us

profile of v2, /device:TPU:0, one launch (start us, length us, event | category | flops | bytes accessed | tf_op | source)
XLA Modules:
  0.0 23.7 jit_solution(8517857502053762792)
XLA Ops:
  0.6 22.4 %layer.1 = (bf16[4,4,512]{2,1,0:T(4,128)(2,1)S(1)}, bf16[4,4,512]{2,1,0:T(4,128)(2,1)S(1)}, bf16[4,4,512]{2,1,0:T(4,128)(2,1)S(1)}, bf16[4,4,512]{2,1,0:T(4,128)(2,1)S(1)}) custom-call(s32[4]{0:T(128)} %len_hbm.1, bf16[4,4,2048]{2,1,0:T(4,128)(2,1)} %x_hbm.1, bf16[3,2048,512]{2,1,0:T(8,128)(2,1)} %wqkv_hbm.1, bf16[512,2048]{1,0:T(8,128)(2,1)} %wout_hbm.1, ...), custom_call_target="tpu_custom_call" | custom-call | tf_op jit(solution)/shard_map/layer/pallas_call | solution.py:414
  23.0 0.7 %deliver.1 = (bf16[4,4,512]{2,1,0:T(4,128)(2,1)}, bf16[4,4,512]{2,1,0:T(4,128)(2,1)}, bf16[4,4,512]{2,1,0:T(4,128)(2,1)}, bf16[4,4,512]{2,1,0:T(4,128)(2,1)}) custom-call(bf16[4,4,512]{2,1,0:T(4,128)(2,1)S(1)} %get-tuple-element.8.refs_0_, bf16[4,4,512]{2,1,0:T(4,128)(2,1)S(1)} %get-tuple-element.9.refs_1_, ...), custom_call_target="tpu_custom_call" | custom-call | tf_op jit(solution)/shard_map/deliver/pallas_call | solution.py:461

commit v3 on v0

--- a/solution.py
+++ b/solution.py
@@ -29,6 +29,20 @@
 
 def iota(shape, axis):
     return lax.broadcasted_iota(jnp.int32, shape, axis)
+
+
+def far_first(me, count):
+    if count > 8 or count & (count - 1):
+        return None
+    order = []
+    for k in range(count - 1, -1, -1):
+        peer, bit = me, 1
+        while bit < count:
+            if k & bit:
+                peer = peer + bit * (1 - 2 * lax.rem(me // bit, 2))
+            bit *= 2
+        order.append(peer)
+    return order
 
 
 def layer_norm(values):
@@ -65,6 +79,16 @@
     pack = own * heads
     me = lax.axis_index("seq")
     mp = lax.axis_index("mp")
+
+    order = far_first(me, S)
+
+    def to_seq(act, me_too):
+        count = S if me_too else S - 1
+        if order is None:
+            each(count, lambda i: act(lax.rem(me + 1 + i, S)))
+        else:
+            for peer in order[:count]:
+                act(peer)
 
     x_copy = pltpu.make_async_copy(x_hbm, x_in, xsem.at[0])
     len_copy = pltpu.make_async_copy(len_hbm, len_ref, xsem.at[1])
@@ -205,7 +229,7 @@
             device_id={axis: slot}, device_id_type=MESH,
         )
 
-    each(S - 1, lambda o: copy1(lax.rem(me + 1 + o, S)).start())
+    to_seq(lambda peer: copy1(peer).start(), False)
     recv1[me] = send1[me]
 
     up_copy.start()
@@ -334,9 +358,9 @@
     for o in others:
         j = lax.rem(mp + o, M)
         send3[j] = down_block(j).astype(BF16)
-        each(S, lambda i: copy3(lax.rem(me + S // 2 + i, S), j).start())
+        to_seq(lambda peer: copy3(peer, j).start(), True)
     send3[mp] = (down_block(mp) + mids[mp]).astype(BF16)
-    each(S - 1, lambda i: copy3(lax.rem(me + 1 + i, S), mp).start())
+    to_seq(lambda peer: copy3(peer, mp).start(), False)
     recv3[me, mp] = send3[mp]
     all_blocks(lambda seq, j: came3(seq, j).wait_recv())
     for i in range(S):

time: 23.6 us -> 23.3 us (0.987)
  Pallas kernels: 22.8 us -> 22.5 us
    pallas_call x1, Pallas kernels: 22.1 us -> 21.8 us  [per_device(): pl.pallas_call(functools.partial(kernel, S, M), out_shape=[pltpu.VMEM(sha...]
where the time goes in v3:
time: 23.3 us; the launch traced here: 23.1 us
  Pallas kernels  22.5 us (97%)
  between operations  0.64 us (3%)
    pallas_call x1, Pallas kernels, per_device(): pl.pallas_call(functools.partial(kernel, S, M), out_shape=[pltpu.VMEM(sha...  21.8 us
    pallas_call x1, Pallas kernels, per_device(): pl.pallas_call(deliver, out_shape=[jax.ShapeDtypeStruct(shape, BF16)] * 4...  0.66 us

profile of v3, /device:TPU:0, one launch (start us, length us, event | category | flops | bytes accessed | tf_op | source)
XLA Modules:
  0.0 23.1 jit_solution(17139320735287936036)
XLA Ops:
  0.6 21.8 %layer.1 = (bf16[4,4,512]{2,1,0:T(4,128)(2,1)S(1)}, bf16[4,4,512]{2,1,0:T(4,128)(2,1)S(1)}, bf16[4,4,512]{2,1,0:T(4,128)(2,1)S(1)}, bf16[4,4,512]{2,1,0:T(4,128)(2,1)S(1)}) custom-call(s32[4]{0:T(128)} %len_hbm.1, bf16[4,4,2048]{2,1,0:T(4,128)(2,1)} %x_hbm.1, bf16[3,2048,512]{2,1,0:T(8,128)(2,1)} %wqkv_hbm.1, bf16[512,2048]{1,0:T(8,128)(2,1)} %wout_hbm.1, ...), custom_call_target="tpu_custom_call" | custom-call | tf_op jit(solution)/shard_map/layer/pallas_call | solution.py:404
  22.5 0.7 %deliver.1 = (bf16[4,4,512]{2,1,0:T(4,128)(2,1)}, bf16[4,4,512]{2,1,0:T(4,128)(2,1)}, bf16[4,4,512]{2,1,0:T(4,128)(2,1)}, bf16[4,4,512]{2,1,0:T(4,128)(2,1)}) custom-call(bf16[4,4,512]{2,1,0:T(4,128)(2,1)S(1)} %get-tuple-element.8.refs_0_, bf16[4,4,512]{2,1,0:T(4,128)(2,1)S(1)} %get-tuple-element.9.refs_1_, ...), custom_call_target="tpu_custom_call" | custom-call | tf_op jit(solution)/shard_map/deliver/pallas_call | solution.py:451
